TPU v7x, 128 devices: a whole 4x4x4 slice. The times are simulated.
128 devices in a mesh: face: 8 (over z_lo, x), tile: 16 (over z_hi, y, core).
Axes of the slice: x: 4, y: 4, z: 4 (z_hi: 2, z_lo: 2; z = z_hi * 2 + z_lo), core: 2. Of those that a mesh axis runs over, the one named last changes fastest.
Arguments:
- source: bfloat16 [8192, 16, 128], P(('face', 'tile')), may hold values from -6 to 6
- entry_block: int32 [16384], P(('face', 'tile')), may hold values from 0 to 16383, as said below
- entry_source: int32 [16384], P(('face', 'tile')), may hold values from 0 to 63
- entry_weight: bfloat16 [16384, 128, 128], P(('face', 'tile')), may hold values from -0.5 to 0.5
- lat_to_nested: int32 [16384], P(('face', 'tile')), may hold values from 0 to 16383, as said below
- face_links: int32 [8, 4, 3], replicated, may hold values from 0 to 7, as said below
- w_in: bfloat16 [16, 90], replicated, may hold values from -1.5 to 1.5
- b_in: float32 [90], replicated, may hold values from -3 to 3
- kernel: float32 [9, 90], replicated, may hold values from -2 to 2
- ln_gain: float32 [90], replicated, may hold values from 0.1 to 1.9
- ln_bias: float32 [90], replicated, may hold values from -3 to 3
- w_one: bfloat16 [90, 360], replicated, may hold values from -0.625 to 0.625
- b_one: float32 [360], replicated, may hold values from -3 to 3
- w_two: bfloat16 [360, 90], replicated, may hold values from -0.3125 to 0.3125
- b_two: float32 [90], replicated, may hold values from -3 to 3
- cotangent: bfloat16 [8, 90, 512, 512], P('face', None, 'tile'), may hold values from -6 to 6
Outputs:
- output: bfloat16 [8, 90, 512, 512], P('face', None, 'tile')
- grad_one: float32 [90, 360], replicated
- grad_two: float32 [360, 90], replicated
- grad_kernel: float32 [9, 90], replicated
Inputs may be any that keep to these rules, and one draw needn't show every extreme that they name: `entry_block`: blocks k * 128 to (k + 1) * 128 - 1 belong to device k. At most 2 entries of one device name blocks of one device; in every draw one device gets exactly 2 from every device. `lat_to_nested`: A permutation of all blocks; the 128 blocks of each device go one to each device. `face_links`: entry [f, s, 0] names a face other than f; [f, s, 1] a side 0 to 3; [f, s, 2] is 0 or 1.
All inputs are finite; a program needn't handle non-finite values.
Results may differ from a plain program's by a relative error of at most 0.0081.
Values may be sent and summed in bfloat16 or wider, within the bound.
A program may use at most 192 MiB of HBM per device.

v0:
```python
import math
import jax
import jax.numpy as jnp
from jax import lax
from jax.sharding import PartitionSpec as P

CAP = 2
GELU_K = 0.7978845608028654
GELU_C = 0.044715
NORM_EPS = 1e-06


def with_halo(cells, sides, width):
    for axis, dim in sides:
        count = lax.axis_size(axis)
        ends = count - 1
        head = lax.slice_in_dim(cells, 0, width, axis=dim)
        tail = lax.slice_in_dim(cells, cells.shape[dim] - width, cells.shape[dim], axis=dim)
        cells = jnp.concatenate(
            [
                lax.ppermute(tail, axis, [(i, (i + 1) % count) for i in range(ends)]),
                cells,
                lax.ppermute(head, axis, [((i + 1) % count, i) for i in range(ends)]),
            ],
            axis=dim,
        )
    return cells


def gelu_pair(pre_act):
    inner = GELU_K * (pre_act + GELU_C * pre_act * pre_act * pre_act)
    tanh_val = jnp.tanh(inner)
    gelu_val = 0.5 * pre_act * (1.0 + tanh_val)
    gelu_slope = 0.5 * (1.0 + tanh_val) + 0.5 * pre_act * (1.0 - tanh_val * tanh_val) * GELU_K * (
        1.0 + 3.0 * GELU_C * pre_act * pre_act
    )
    return (gelu_val, gelu_slope)


def contract_rows(left_mat, right_mat):
    return lax.dot_general(
        left_mat, right_mat, (((1,), (1,)), ((), ())), preferred_element_type=jnp.float32
    )


def strip_work(padded, middle, cotan, kernel, ln_gain, ln_bias, w_one, b_one, w_two, b_two, scale):
    lat_count = padded.shape[0]
    row_count = padded.shape[1] - 2
    col_count = padded.shape[2] - 2
    wide = padded.astype(jnp.float32)
    depth_sum = jnp.zeros((lat_count, row_count, col_count), jnp.float32)
    for tap_index in range(9):
        row_off = tap_index // 3
        col_off = tap_index % 3
        window = wide[:, row_off : row_off + row_count, col_off : col_off + col_count]
        depth_sum = depth_sum + kernel[tap_index][:, None, None] * window
    flat = depth_sum.reshape(lat_count, row_count * col_count)
    mean_val = jnp.mean(flat, axis=0, keepdims=True)
    centered = flat - mean_val
    variance = jnp.mean(centered * centered, axis=0, keepdims=True)
    inv_std = lax.rsqrt(variance + NORM_EPS)
    scaled = centered * inv_std
    normed = (scaled * ln_gain[:, None] + ln_bias[:, None]).astype(jnp.bfloat16)
    pre_act = jnp.dot(w_one.T, normed, preferred_element_type=jnp.float32) + b_one[:, None]
    gelu_val, gelu_slope = gelu_pair(pre_act)
    hidden = gelu_val.astype(jnp.bfloat16)
    summed = (
        jnp.dot(w_two.T, hidden, preferred_element_type=jnp.float32)
        + b_two[:, None]
        + middle.reshape(lat_count, -1).astype(jnp.float32)
    )
    output = summed.astype(jnp.bfloat16).reshape(lat_count, row_count, col_count)
    cot_flat = cotan.reshape(lat_count, -1)
    grad_two = contract_rows(hidden, cot_flat) * scale
    back_hidden = jnp.dot(w_two, cot_flat, preferred_element_type=jnp.float32)
    back_pre = (back_hidden * gelu_slope).astype(jnp.bfloat16)
    grad_one = contract_rows(normed, back_pre) * scale
    back_hat = jnp.dot(w_one, back_pre, preferred_element_type=jnp.float32) * ln_gain[:, None]
    back_depth = inv_std * (
        back_hat
        - jnp.mean(back_hat, axis=0, keepdims=True)
        - scaled * jnp.mean(back_hat * scaled, axis=0, keepdims=True)
    )
    back_grid = back_depth.reshape(lat_count, row_count, col_count)
    kernel_rows = []
    for tap_index in range(9):
        row_off = tap_index // 3
        col_off = tap_index % 3
        window = wide[:, row_off : row_off + row_count, col_off : col_off + col_count]
        kernel_rows.append(jnp.sum(back_grid * window, axis=(1, 2)))
    grad_kernel = jnp.stack(kernel_rows, axis=0) * scale
    return (output, grad_one, grad_two, grad_kernel)


def lift(w_in, b_in, values):
    flat = values.reshape(values.shape[0], -1)
    mixed = jnp.dot(w_in.T, flat, preferred_element_type=jnp.float32) + b_in[:, None]
    return mixed.astype(jnp.bfloat16).reshape((w_in.shape[1],) + values.shape[1:])


def assemble(rows_part, cols_part):
    tile_count = rows_part.shape[0]
    chan_count = rows_part.shape[1]
    left_line = cols_part[:, 0].transpose(1, 0, 2).reshape(chan_count, -1)
    right_line = cols_part[:, 1].transpose(1, 0, 2).reshape(chan_count, -1)
    return jnp.stack([rows_part[0], rows_part[tile_count - 1], left_line, right_line], axis=0)


def per_device(
    source,
    entry_block,
    entry_source,
    entry_weight,
    lat_to_nested,
    face_links,
    w_in,
    b_in,
    kernel,
    ln_gain,
    ln_bias,
    w_one,
    b_one,
    w_two,
    b_two,
    cotangent,
):
    tile_count = lax.axis_size("tile")
    tile_at = lax.axis_index("tile")
    face_at = lax.axis_index("face")
    face_count = lax.axis_size("face")
    dev_count = lax.axis_size(("face", "tile"))
    in_count = source.shape[1]
    block_len = entry_weight.shape[2]
    row_count = cotangent.shape[2]
    line_len = cotangent.shape[3]
    chosen = jnp.take(source, entry_source, axis=0)
    partials = jnp.einsum(
        "eis,esp->eip", chosen, entry_weight, preferred_element_type=jnp.float32
    ).astype(jnp.bfloat16)
    owner_dev = entry_block // dev_count
    local_block = entry_block % dev_count
    hit_table = (owner_dev[:, None] == jnp.arange(dev_count, dtype=jnp.int32)[None, :]).astype(
        jnp.int32
    )
    slot_rank = jnp.sum((jnp.cumsum(hit_table, axis=0) - 1) * hit_table, axis=1)
    outbox = (
        jnp.zeros((dev_count, CAP, in_count, block_len), jnp.bfloat16)
        .at[owner_dev, slot_rank]
        .set(partials)
    )
    labels = (
        jnp.full((dev_count, CAP), dev_count, jnp.int32).at[owner_dev, slot_rank].set(local_block)
    )
    received, got_labels = (
        lax.all_to_all(outbox, ("face", "tile"), split_axis=0, concat_axis=0, tiled=True),
        lax.all_to_all(labels, ("face", "tile"), split_axis=0, concat_axis=0, tiled=True),
    )
    lat_sum = jnp.zeros((dev_count, in_count, block_len), jnp.float32)
    lat_sum = lat_sum.at[got_labels.reshape(-1)].add(
        received.reshape(-1, in_count, block_len).astype(jnp.float32), mode="drop"
    )
    lat_field = lat_sum.astype(jnp.bfloat16)
    target_dev = lat_to_nested // dev_count
    target_spot = lat_to_nested % dev_count
    outgoing = jnp.zeros_like(lat_field).at[target_dev].set(lat_field)
    out_spots = jnp.zeros((dev_count,), jnp.int32).at[target_dev].set(target_spot)
    incoming, in_spots = (
        lax.all_to_all(outgoing, ("face", "tile"), split_axis=0, concat_axis=0, tiled=True),
        lax.all_to_all(out_spots, ("face", "tile"), split_axis=0, concat_axis=0, tiled=True),
    )
    placed = jnp.zeros_like(incoming).at[in_spots].set(incoming)
    inputs_tile = placed.transpose(1, 0, 2).reshape(in_count, row_count, line_len)
    latent = lift(w_in, b_in, inputs_tile)
    chan_count = latent.shape[0]
    row_start = tile_at * row_count
    edge_cols = jnp.stack([latent[:, :, 0], latent[:, :, line_len - 1]], axis=0)
    edge_row = jnp.where(tile_at == 0, latent[:, 0, :], latent[:, row_count - 1, :])
    rows_face, cols_face = (
        lax.all_gather(edge_row.reshape(-1), "tile", axis=0, tiled=True),
        lax.all_gather(edge_cols.reshape(-1), "tile", axis=0, tiled=True),
    )
    own_lines = assemble(
        rows_face.reshape(tile_count, chan_count, line_len),
        cols_face.reshape(tile_count, 2, chan_count, row_count),
    )
    all_lines = lax.all_gather(own_lines.reshape(-1), "face", axis=0, tiled=True).reshape(
        face_count, 4, chan_count, line_len
    )
    face_link = face_links[face_at]
    picked = all_lines[face_link[:, 0], face_link[:, 1]]
    picked = jnp.where(face_link[:, 2][:, None, None] == 1, picked[:, :, ::-1], picked)
    row_lines = picked[0:2]
    full_cols = jnp.pad(picked[2:4], ((0, 0), (0, 0), (1, 1)))
    side_cols = lax.dynamic_slice_in_dim(full_cols, row_start, row_count + 2, 2)
    rim = jnp.stack([latent[:, 0, :], latent[:, row_count - 1, :]], axis=1)
    extended = with_halo(rim, (("tile", 1),), 1)
    upper_row = extended[:, 0, :]
    lower_row = extended[:, 3, :]
    spot_ids = jnp.arange(row_count + 2, dtype=jnp.int32) + row_start - 1
    inside = (spot_ids >= 0) & (spot_ids < line_len)
    side_cols = jnp.where(inside[None, None, :], side_cols, jnp.zeros_like(side_cols))
    top_row = jnp.where(tile_at == 0, row_lines[0], upper_row)
    bottom_row = jnp.where(tile_at == tile_count - 1, row_lines[1], lower_row)
    middle = jnp.concatenate([top_row[:, None, :], latent, bottom_row[:, None, :]], axis=1)
    padded = jnp.concatenate([side_cols[0][:, :, None], middle, side_cols[1][:, :, None]], axis=2)
    scale = 1.0 / math.sqrt(face_count * line_len * line_len)
    output, grad_one, grad_two, grad_kernel = strip_work(
        padded, latent, cotangent[0], kernel, ln_gain, ln_bias, w_one, b_one, w_two, b_two, scale
    )
    grad_one, grad_two, grad_kernel = lax.psum((grad_one, grad_two, grad_kernel), ("face", "tile"))
    return (output[None], grad_one, grad_two, grad_kernel)


def solution(mesh):
    placed = (
        P(("face", "tile"), None, None),
        P(("face", "tile")),
        P(("face", "tile")),
        P(("face", "tile"), None, None),
        P(("face", "tile")),
        P(),
        P(),
        P(),
        P(),
        P(),
        P(),
        P(),
        P(),
        P(),
        P(),
        P("face", None, "tile", None),
    )
    return jax.shard_map(
        per_device,
        mesh=mesh,
        in_specs=placed,
        out_specs=(P("face", None, "tile", None), P(), P(), P()),
        check_vma=False,
    )
```

profile of v0, /device:TPU:1, one launch (start us, length us, event | category | flops | bytes accessed | tf_op | source)
XLA Modules:
  0.0 591.9 jit_solution(9418654939937501962)
XLA Ops:
  15.5 11.5 %all-to-all-start.1 = ((s32[128,1,2]{2,1,0:T(1,128)}), s32[128,1,2]{2,1,0:T(1,128)S(1)}, u32[]{:S(2)}, u32[]{:S(2)}) async-start(s32[128,1,2]{2,1,0:T(1,128)} %copy.79), calls=%async_computation.1 | async-start | bytes 131072 | tf_op jit(solution)/shard_map/all_to_all | solution.py:156
  33.0 13.3 %scatter_fusion.1 = bf16[128,2,16,128]{3,2,1,0:T(8,128)(2,1)} fusion(bf16[128,2,16,128]{3,2,1,0:T(8,128)(2,1)} %broadcast_in_dim.46, s32[128]{0:T(128)S(1)} %fusion.33, bf16[128,16,128]{2,1,0:T(8,128)(2,1)S(1)} %convolution_convert_fusion), kind=kCustom, calls=%fused_computation.4 | custom fusion | bytes 1573888 | tf_op jit(solution)/shard_map/scatter | solution.py:149
  46.2 9.8 %all-to-all-start.2 = ((bf16[128,2,16,128]{3,2,1,0:T(8,128)(2,1)}), bf16[128,2,16,128]{3,2,1,0:T(8,128)(2,1)S(1)}, u32[]{:S(2)}, u32[]{:S(2)}) async-start(bf16[128,2,16,128]{3,2,1,0:T(8,128)(2,1)} %scatter_fusion.1), calls=%async_computation.2 | async-start | bytes 2097152 | tf_op jit(solution)/shard_map/all_to_all | solution.py:155
  59.2 15.7 %all-to-all-done.2 = bf16[128,2,16,128]{3,2,1,0:T(8,128)(2,1)S(1)} async-done(((bf16[128,2,16,128]{3,2,1,0:T(8,128)(2,1)}), bf16[128,2,16,128]{3,2,1,0:T(8,128)(2,1)S(1)}, u32[]{:S(2)}, u32[]{:S(2)}) %all-to-all-start.2) | async-done | bytes 1048608 | tf_op jit(solution)/shard_map/all_to_all | solution.py:155
  79.8 9.2 %scatter_fusion.2 = f32[128,16,128]{2,1,0:T(8,128)S(1)} fusion(f32[128,16,128]{2,1,0:T(8,128)S(1)} %broadcast_in_dim.43, s32[256]{0:T(256)S(1)} %bitcast.183, f32[256,16,128]{2,1,0:T(8,128)S(1)} %bitcast_convert_fusion), kind=kCustom, calls=%fused_computation.5 | custom fusion | flops 524288 | bytes 6292480 | tf_op jit(solution)/shard_map/scatter-add | solution.py:159
  90.0 13.2 %scatter_fusion.3 = bf16[128,16,128]{2,1,0:T(8,128)(2,1)} fusion(bf16[128,16,128]{2,1,0:T(8,128)(2,1)} %broadcast.194.clone, s32[128]{0:T(128)S(1)} %get-tuple-element.46, bf16[128,16,128]{2,1,0:T(8,128)(2,1)S(1)} %convert_element_type.45), kind=kCustom, calls=%fused_computation.6 | custom fusion | bytes 1573376 | tf_op jit(solution)/shard_map/scatter | solution.py:165
  103.1 9.8 %all-to-all-start.3 = ((bf16[128,16,128]{2,1,0:T(8,128)(2,1)}), bf16[128,16,128]{2,1,0:T(8,128)(2,1)S(1)}, u32[]{:S(2)}, u32[]{:S(2)}) async-start(bf16[128,16,128]{2,1,0:T(8,128)(2,1)} %scatter_fusion.3), calls=%async_computation.3 | async-start | bytes 1048576 | tf_op jit(solution)/shard_map/all_to_all | solution.py:168
  115.8 10.7 %all-to-all-done.3 = bf16[128,16,128]{2,1,0:T(8,128)(2,1)S(1)} async-done(((bf16[128,16,128]{2,1,0:T(8,128)(2,1)}), bf16[128,16,128]{2,1,0:T(8,128)(2,1)S(1)}, u32[]{:S(2)}, u32[]{:S(2)}) %all-to-all-start.3) | async-done | bytes 524320 | tf_op jit(solution)/shard_map/all_to_all | solution.py:168
  127.4 13.2 %scatter_fusion.4 = bf16[128,16,128]{2,1,0:T(8,128)(2,1)} fusion(bf16[128,16,128]{2,1,0:T(8,128)(2,1)} %broadcast.194, s32[128]{0:T(128)S(1)} %fusion.31, bf16[128,16,128]{2,1,0:T(8,128)(2,1)S(1)} %all-to-all-done.3), kind=kCustom, calls=%fused_computation.7 | custom fusion | bytes 1573376 | tf_op jit(solution)/shard_map/scatter | solution.py:171
  154.1 23.3 %all-gather = bf16[16,1,5760]{2,1,0:T(2,128)(2,1)} all-gather(bf16[1,1,5760]{2,1,0:T(2,128)(2,1)S(1)} %reshape.282), channel_id=1, replica_groups=mesh['face'=8,'tile'=16] {'tile'}, dimensions={0}, use_global_device_ids=true | all-gather | bytes 195840 | tf_op jit(solution)/shard_map/all_gather | solution.py:180
  214.0 24.0 %all-gather.6.cloned.1.call-done = bf16[1474560]{0:T(1024)(128)(2,1)} async-done(((bf16[184320]{0:T(1024)(128)(2,1)}), bf16[1474560]{0:T(1024)(128)(2,1)}) %all-gather.6.cloned.1.call-update) | async-done | bytes 2949136 | tf_op jit(solution)/shard_map/all_gather | solution.py:186
  246.8 8.5 %rev.3 = bf16[4,90,512]{2,1,0:T(8,128)(2,1)} reverse(bf16[4,90,512]{2,1,0:T(8,128)(2,1)} %gather_fusion.1), dimensions={2} | reverse | bytes 737280 | tf_op jit(solution)/shard_map/rev | solution.py:191
  262.7 8.9 %maximum_convert_fusion = f32[90,34,514]{2,1,0:T(8,128)} fusion(bf16[90,34,1]{2,1,0:T(8,128)(2,1)} %copy.94, bf16[90,1,512]{2,1,0:T(2,128)(2,1)S(1)} %copy.91, bf16[90,32,512]{2,1,0:T(8,128)(2,1)} %slice.204, bf16[90,1,512]{2,1,0:T(2,128)(2,1)} %copy.90, bf16[90,34,1]{2,1,0:T(8,128)(2,1)} %copy.93), kind=kLoop, calls=%fused_computation.45 | loop fusion | flops 15728400 | bytes 9437040 | tf_op jit(solution)/shard_map/convert_element_type | solution.py:50
  271.6 34.9 %fusion.38 = (f32[32,512]{1,0:T(8,128)S(1)}, f32[90,32,512]{2,1,0:T(8,128)}) fusion(f32[90,34,514]{2,1,0:T(8,128)} %maximum_convert_fusion, f32[90]{0:T(128)S(1)} %get-tuple-element.41, f32[90]{0:T(128)S(1)} %get-tuple-element.42, f32[90]{0:T(128)S(1)} %get-tuple-element.35, f32[90]{0:T(128)S(1)} %get-tuple-element.36, f32[90]{0:T(128)S(1)} %get-tuple-element.37, ...), kind=kLoop, calls=%fused_computation.128 | loop fusion | flops 26525696 | bytes 59051176 | tf_op jit(solution)/shard_map/reduce_sum | solution.py:58
  315.5 15.2 %multiply_convert_fusion = (bf16[360,16384]{1,0:T(8,128)(2,1)}, f32[16384,360]{0,1:T(8,128)}) fusion(f32[360]{0:T(512)S(1)} %copy-done.16, bf16[90,360]{1,0:T(8,128)(2,1)S(1)} %copy-done.7, f32[90,16384]{1,0:T(8,128)S(1)} %bitcast.150, f32[90]{0:T(128)S(1)} %copy-done.15, f32[90]{0:T(128)S(1)} %copy-done.10, f32[16384]{0:T(1024)S(1)} %bitcast.169, ...), kind=kOutput, calls=%fused_computation.18 | convolution fusion | flops 1128038400 | bytes 41485712 | tf_op jit(solution)/shard_map/dot_general | solution.py:64
  330.7 20.6 %fusion.6 = bf16[360,16384]{1,0:T(8,128)(2,1)} fusion(f32[16384,360]{0,1:T(8,128)} %get-tuple-element.48, bf16[360,90]{0,1:T(8,128)(2,1)S(1)} %copy-done.8, bf16[90,16384]{1,0:T(8,128)(2,1)S(1)} %bitcast.165), kind=kOutput, calls=%fused_computation.16 | convolution fusion | flops 1173749760 | bytes 38403360 | tf_op jit(solution)/shard_map/dot_general | solution.py:75
  351.3 8.7 %convolution_multiply_fusion.1 = f32[90,360]{1,0:T(8,128)} fusion(bf16[360,16384]{1,0:T(8,128)(2,1)} %fusion.6, f32[90,16384]{1,0:T(8,128)S(1)} %bitcast.151, f32[90]{0:T(128)S(1)} %copy-done.15, f32[90]{0:T(128)S(1)} %copy-done.10, f32[16384]{0:T(1024)S(1)} %bitcast.170, f32[16384]{0:T(1024)S(1)} %bitcast.174), kind=kOutput, calls=%fused_computation.48 | convolution fusion | flops 1069088384 | bytes 17956112 | tf_op jit(solution)/shard_map/dot_general | solution.py:41
  360.0 10.5 %fusion.13 = (f32[16384]{0:T(1024)S(1)}, f32[16384,90]{0,1:T(8,128)}) fusion(f32[90,16384]{1,0:T(8,128)S(1)} %bitcast.152, f32[16384]{0:T(1024)S(1)} %bitcast.171, f32[16384]{0:T(1024)S(1)} %bitcast.175, f32[90]{0:T(128)S(1)} %copy-done.10, bf16[360,16384]{1,0:T(8,128)(2,1)} %fusion.6, bf16[90,360]{1,0:T(8,128)(2,1)S(1)} %copy-done.7), kind=kOutput, calls=%fused_computation.31 | convolution fusion | flops 1069039616 | bytes 23854728 | tf_op jit(solution)/shard_map/dot_general | solution.py:78
  370.6 8.6 %convolution_multiply_fusion.2 = f32[360,90]{0,1:T(8,128)} fusion(bf16[360,16384]{1,0:T(8,128)(2,1)} %get-tuple-element.47, bf16[90,16384]{1,0:T(8,128)(2,1)S(1)} %bitcast.166), kind=kOutput, calls=%fused_computation.49 | convolution fusion | flops 1061715584 | bytes 14875200 | tf_op jit(solution)/shard_map/dot_general | solution.py:41
  379.1 6.9 %fusion.10 = bf16[90,16384]{1,0:T(8,128)(2,1)S(1)} fusion(bf16[360,16384]{1,0:T(8,128)(2,1)} %get-tuple-element.47, bf16[360,90]{0,1:T(8,128)(2,1)S(1)} %copy-done.8, bf16[16384,90]{0,1:T(8,128)(2,1)S(1)} %fusion.7, f32[90]{0:T(128)S(1)} %copy-done.11), kind=kOutput, calls=%fused_computation.26 | convolution fusion | flops 1067581440 | bytes 17759880 | tf_op jit(solution)/shard_map/dot_general | solution.py:68
  398.9 7.0 %copy.108 = f32[12,8,32,512]{3,2,1,0:T(8,128)} copy(f32[12,8,32,512]{3,1,2,0:T(8,128)S(1)} %bitcast.158) | data formatting | bytes 12582912
  405.9 31.9 %multiply_reduce_fusion = (f32[90]{0:T(128)S(1)}, f32[90]{0:T(128)S(1)}, f32[90]{0:T(128)S(1)}, f32[90]{0:T(128)S(1)}, f32[90]{0:T(128)S(1)}, /*index=5*/f32[90]...) fusion(f32[90,34,514]{2,1,0:T(8,128)} %maximum_convert_fusion, f32[96,32,512]{2,1,0:T(8,128)} %bitcast.159), kind=kLoop, calls=%fused_computation.34 | loop fusion | flops 26541270 | bytes 58985640 | tf_op jit(solution)/shard_map/reduce_sum | solution.py:90
  437.8 67.0 %psum.23 = f32[9,90]{1,0:T(8,128)} all-reduce(f32[9,90]{1,0:T(8,128)S(1)} %broadcast_multiply_fusion.3), channel_id=1, replica_groups=mesh['face'=8,'tile'=16] {'face','tile'}, use_global_device_ids=true, to_apply=%region_23.24 | all-reduce | flops 810 | bytes 6480 | tf_op jit(solution)/shard_map/psum | solution.py:210
  504.8 77.2 %all-reduce.4.cloned.1.call-done = (f32[90,360]{1,0:T(8,128)}, f32[360,90]{0,1:T(8,128)}) async-done(((f32[90,360]{1,0:T(8,128)}, f32[360,90]{0,1:T(8,128)}), (f32[90,360]{1,0:T(8,128)}, f32[360,90]{0,1:T(8,128)})) %all-reduce.4.cloned.1.call-update) | async-done | bytes 259216 | tf_op jit(solution)/shard_map/psum | solution.py:210
  (142 shorter events, 117.9 us)
Async XLA Ops:
  7.2 20.5 %copy-start = (bf16[64,16,128]{2,1,0:T(8,128)(2,1)S(1)}, bf16[64,16,128]{2,1,0:T(8,128)(2,1)}, u32[]{:S(2)}) copy-start(bf16[64,16,128]{2,1,0:T(8,128)(2,1)} %param.16) | copy-start | bytes 786436
  8.0 48.0 %copy-start.17 = (s32[128]{0:T(128)S(1)}, s32[128]{0:T(128)}, u32[]{:S(2)}) copy-start(s32[128]{0:T(128)} %param.20) | copy-start | bytes 1540
  15.5 30.7 %all-to-all-start.1 = ((s32[128,1,2]{2,1,0:T(1,128)}), s32[128,1,2]{2,1,0:T(1,128)S(1)}, u32[]{:S(2)}, u32[]{:S(2)}) async-start(s32[128,1,2]{2,1,0:T(1,128)} %copy.79), calls=%async_computation.1 | async-start | bytes 131072 | tf_op jit(solution)/shard_map/all_to_all | solution.py:156
  46.2 28.7 %all-to-all-start.2 = ((bf16[128,2,16,128]{3,2,1,0:T(8,128)(2,1)}), bf16[128,2,16,128]{3,2,1,0:T(8,128)(2,1)S(1)}, u32[]{:S(2)}, u32[]{:S(2)}) async-start(bf16[128,2,16,128]{3,2,1,0:T(8,128)(2,1)} %scatter_fusion.1), calls=%async_computation.2 | async-start | bytes 2097152 | tf_op jit(solution)/shard_map/all_to_all | solution.py:155
  74.9 28.2 %all-to-all-start = ((s32[128,1,1]{2,1,0:T(1,128)}), s32[128,1,1]{2,1,0:T(1,128)S(1)}, u32[]{:S(2)}, u32[]{:S(2)}) async-start(s32[128,1,1]{2,1,0:T(1,128)} %copy.78), calls=%async_computation | async-start | bytes 131072 | tf_op jit(solution)/shard_map/all_to_all | solution.py:169
  79.8 60.8 %copy-start.12 = (bf16[16,90]{1,0:T(8,128)(2,1)S(1)}, bf16[16,90]{1,0:T(8,128)(2,1)}, u32[]{:S(2)}) copy-start(bf16[16,90]{1,0:T(8,128)(2,1)} %param.22) | copy-start | bytes 8644
  79.8 60.8 %copy-start.14 = (f32[90]{0:T(128)S(1)}, f32[90]{0:T(128)}, u32[]{:S(2)}) copy-start(f32[90]{0:T(128)} %param.23) | copy-start | bytes 1084
  103.1 23.4 %all-to-all-start.3 = ((bf16[128,16,128]{2,1,0:T(8,128)(2,1)}), bf16[128,16,128]{2,1,0:T(8,128)(2,1)S(1)}, u32[]{:S(2)}, u32[]{:S(2)}) async-start(bf16[128,16,128]{2,1,0:T(8,128)(2,1)} %scatter_fusion.3), calls=%async_computation.3 | async-start | bytes 1048576 | tf_op jit(solution)/shard_map/all_to_all | solution.py:168
  113.0 77.5 %all-gather.4.cloned.1.call-start = ((), (), s32[]{:S(2)}) async-start(), calls=%async_computation.4 | async-start | bytes 1566720 | tf_op jit(solution)/shard_map/all_gather | solution.py:179
  143.9 1.7 copy-start.3
  146.5 52.0 %copy-start.9 = (s32[8,4,3]{0,1,2:T(4,128)S(1)}, s32[8,4,3]{0,1,2:T(4,128)}, u32[]{:S(2)}) copy-start(s32[8,4,3]{0,1,2:T(4,128)} %param.21) | copy-start | bytes 1156
  147.3 90.7 %all-gather.6.cloned.1.call-start = ((), (), s32[]{:S(2)}) async-start(), calls=%async_computation.5 | async-start | bytes 3317760 | tf_op jit(solution)/shard_map/all_gather | solution.py:186
  198.3 6.8 %copy-start.13 = (f32[9,90]{1,0:T(8,128)S(1)}, f32[9,90]{1,0:T(8,128)}, u32[]{:S(2)}) copy-start(f32[9,90]{1,0:T(8,128)} %param.24) | copy-start | bytes 9724
  198.3 383.7 %all-reduce.4.cloned.1.call-start = ((), (), s32[]{:S(2)}) async-start(), calls=%async_computation.6 | async-start | bytes 589824 | tf_op jit(solution)/shard_map/psum | solution.py:210
  209.0 50.1 %collective-permute-start = (bf16[90,1,512]{2,0,1:T(8,128)(2,1)}, bf16[90,1,512]{2,0,1:T(8,128)(2,1)S(1)}, u32[]{:S(2)}, u32[]{:S(2)}) collective-permute-start(bf16[90,1,512]{2,0,1:T(8,128)(2,1)} %get-tuple-element.18), channel_id=1, source_target_pairs={{0,1},{1,2},{2,3},{3,4},{4,5},{5,6},{6,7},{7,8},{8,9},{9,10},{10,1... | collective-permute-start | bytes 276488 | tf_op jit(solution)/shard_map/ppermute | solution.py:21
  212.0 47.1 %collective-permute-start.1 = (bf16[90,1,512]{2,0,1:T(8,128)(2,1)}, bf16[90,1,512]{2,0,1:T(8,128)(2,1)}, u32[]{:S(2)}, u32[]{:S(2)}) collective-permute-start(bf16[90,1,512]{2,0,1:T(8,128)(2,1)} %get-tuple-element.19), channel_id=1, source_target_pairs={{1,0},{2,1},{3,2},{4,3},{5,4},{6,5},{7,6},{8,7},{9,8},{10,9},{11,1... | collective-permute-start | bytes 276488 | tf_op jit(solution)/shard_map/ppermute | solution.py:23
  306.5 8.0 %slice-start = ((s8[5898240]{0:T(1024)(128)(4,1)}), s8[4194304]{0:T(1024)(128)(4,1)S(1)}, s32[]{:S(2)}) async-start(s8[5898240]{0:T(1024)(128)(4,1)} %bitcast.154), calls=%async_computation.7 | async-start | bytes 8388608
  310.1 4.5 slice-start.1
  314.5 45.5 %copy-start.2 = (f32[12,8,32,512]{3,1,2,0:T(8,128)}, f32[12,8,32,512]{3,1,2,0:T(8,128)S(1)}, u32[]{:S(2)}) copy-start(f32[12,8,32,512]{3,1,2,0:T(8,128)S(1)} %copy.103) | copy-start | bytes 18874372
  315.4 15.2 %copy-start.4 = (bf16[12,8,32,512]{3,1,2,0:T(8,128)(2,1)S(1)}, bf16[12,8,32,512]{3,1,2,0:T(8,128)(2,1)}, u32[]{:S(2)}) copy-start(bf16[12,8,32,512]{3,1,2,0:T(8,128)(2,1)} %copy.107) | copy-start | bytes 9437188
  315.4 15.2 %copy-start.8 = (bf16[360,90]{0,1:T(8,128)(2,1)S(1)}, bf16[360,90]{0,1:T(8,128)(2,1)}, u32[]{:S(2)}) copy-start(bf16[360,90]{0,1:T(8,128)(2,1)} %param.29) | copy-start | bytes 194404
  360.0 10.6 %copy-start.5 = (bf16[12,8,32,512]{3,1,2,0:T(8,128)(2,1)S(1)}, bf16[12,8,32,512]{3,1,2,0:T(8,128)(2,1)}, u32[]{:S(2)}) copy-start(bf16[12,8,32,512]{3,1,2,0:T(8,128)(2,1)} %copy.107) | copy-start | bytes 9437188
  370.6 8.6 %copy-start.11 = (f32[90]{0:T(128)S(1)}, f32[90]{0:T(128)}, u32[]{:S(2)}) copy-start(f32[90]{0:T(128)} %param.30) | copy-start | bytes 1084
  405.9 179.2 %copy-start.1 = (bf16[64,16,128]{2,1,0:T(8,128)(2,1)S(1)}, bf16[64,16,128]{2,1,0:T(8,128)(2,1)}, u32[]{:S(2)}) copy-start(bf16[64,16,128]{2,1,0:T(8,128)(2,1)} %param.16) | copy-start | bytes 786436
  (5 other events, 4.5 us)
Sparse Core Ops, SparseCore 0:
  147.4 43.0 all-gather.3
  198.4 39.5 all-gather.5
  437.9 144.0 all-reduce.3
where the time goes:
time: 601 us; the launch traced here: 592 us
  waiting for transfers between devices  132 us (22%)
  local copies, waits for them, and re-layouts  130 us (22%)
  other arithmetic  107 us (18%)
  blocking collectives  90.3 us (15%)
  matrix products  76 us (13%)
  starting transfers between devices  41.3 us (7%)
  between operations  14.6 us (2%)
    psum x1, waiting for transfers between devices, per_device(): lax.psum((grad_one, grad_two, grad_kernel), ('face', 'tile'))  77.2 us
    psum x1, blocking collectives, per_device(): lax.psum((grad_one, grad_two, grad_kernel), ('face', 'tile'))  67 us
    reduce_sum x1, other arithmetic, strip_work(): mean_val = jnp.mean(flat, axis=0, keepdims=True)  34.9 us
    unnamed x54, local copies, waits for them, and re-layouts  33.3 us
    reduce_sum x1, other arithmetic, strip_work(): kernel_rows.append(jnp.sum(back_grid * window, axis=(1, 2)))  31.9 us
    all_gather x1, waiting for transfers between devices, per_device(): lax.all_gather(own_lines.reshape(-1), 'face', axis=0, tiled=True)  24 us
    all_gather x1, blocking collectives, per_device(): lax.all_gather(edge_cols.reshape(-1), 'tile', axis=0, tiled=True)  23.3 us
    dot_general x1, matrix products, strip_work(): back_hidden = jnp.dot(w_two, cot_flat, preferred_element_type=jnp.float32)  20.6 us
  transfers between devices with their start and end apart: 9, of which 5 were waited for; matrix products, arithmetic and copies ran while one was open for 16% of the time, Pallas kernels for 0%

commit v1 on v0

--- a/solution.py
+++ b/solution.py
@@ -207,7 +207,9 @@
     output, grad_one, grad_two, grad_kernel = strip_work(
         padded, latent, cotangent[0], kernel, ln_gain, ln_bias, w_one, b_one, w_two, b_two, scale
     )
-    grad_one, grad_two, grad_kernel = lax.psum((grad_one, grad_two, grad_kernel), ("face", "tile"))
+    grad_one, grad_two, grad_kernel = lax.psum(
+        lax.psum((grad_one, grad_two, grad_kernel), "face"), "tile"
+    )
     return (output[None], grad_one, grad_two, grad_kernel)
 
 

time: 601 us -> 646 us (1.075)
  waiting for transfers between devices: 132 us -> 202 us
  local copies, waits for them, and re-layouts: 130 us -> 117 us
  blocking collectives: 90.3 us -> 78.8 us
    psum x1 -> x2, waiting for transfers between devices: 77.2 us -> 145 us  [the longest x1 137 us: per_device(): lax.psum(lax.psum((grad_one, grad_two, grad_kernel), 'face'), 'tile')]
    psum x1 -> x2, blocking collectives: 67 us -> 55.7 us  [the longest x1 40 us: per_device(): lax.psum(lax.psum((grad_one, grad_two, grad_kernel), 'face'), 'tile')]
    scatter x1, local copies, waits for them, and re-layouts: 13.2 us -> 4.37 us  [per_device(): placed = jnp.zeros_like(incoming).at[in_spots].set(incoming)]
    unnamed x54 -> x58, local copies, waits for them, and re-layouts: 33.3 us -> 33.4 us
  transfers between devices with their start and end apart: 9 -> 10, of which waited for: 5 -> 6; matrix products, arithmetic and copies ran while one was open for 16% -> 16% of each run, Pallas kernels for 0% -> 0%
where the time goes in v1:
time: 646 us; the launch traced here: 636 us
  waiting for transfers between devices  202 us (31%)
  local copies, waits for them, and re-layouts  117 us (18%)
  other arithmetic  106 us (16%)
  blocking collectives  78.8 us (12%)
  matrix products  75 us (12%)
  starting transfers between devices  41.9 us (6%)
  between operations  14.6 us (2%)
    psum x1, waiting for transfers between devices, per_device(): lax.psum(lax.psum((grad_one, grad_two, grad_kernel), 'face'), 'tile')  137 us
    psum x1, blocking collectives, per_device(): lax.psum(lax.psum((grad_one, grad_two, grad_kernel), 'face'), 'tile')  40 us
    reduce_sum x1, other arithmetic, strip_work(): mean_val = jnp.mean(flat, axis=0, keepdims=True)  34.7 us
    unnamed x58, local copies, waits for them, and re-layouts  33.4 us
    reduce_sum x1, other arithmetic, strip_work(): kernel_rows.append(jnp.sum(back_grid * window, axis=(1, 2)))  31.6 us
    all_gather x1, waiting for transfers between devices, per_device(): lax.all_gather(own_lines.reshape(-1), 'face', axis=0, tiled=True)  25.2 us
    all_gather x1, blocking collectives, per_device(): lax.all_gather(edge_cols.reshape(-1), 'tile', axis=0, tiled=True)  23.1 us
    dot_general x1, matrix products, strip_work(): back_hidden = jnp.dot(w_two, cot_flat, preferred_element_type=jnp.float32)  20.7 us
  transfers between devices with their start and end apart: 10, of which 6 were waited for; matrix products, arithmetic and copies ran while one was open for 16% of the time, Pallas kernels for 0%

profile of v1, /device:TPU:1, one launch (start us, length us, event | category | flops | bytes accessed | tf_op | source)
XLA Modules:
  0.0 635.6 jit_solution(14422402901734254733)
XLA Ops:
  15.5 11.5 %all-to-all-start.1 = ((s32[128,1,2]{2,1,0:T(1,128)}), s32[128,1,2]{2,1,0:T(1,128)S(1)}, u32[]{:S(2)}, u32[]{:S(2)}) async-start(s32[128,1,2]{2,1,0:T(1,128)} %copy.79), calls=%async_computation.1 | async-start | bytes 131072 | tf_op jit(solution)/shard_map/all_to_all | solution.py:156
  33.0 13.3 %scatter_fusion.1 = bf16[128,2,16,128]{3,2,1,0:T(8,128)(2,1)} fusion(bf16[128,2,16,128]{3,2,1,0:T(8,128)(2,1)} %broadcast_in_dim.46, s32[128]{0:T(128)S(1)} %fusion.33, bf16[128,16,128]{2,1,0:T(8,128)(2,1)S(1)} %convolution_convert_fusion), kind=kCustom, calls=%fused_computation.4 | custom fusion | bytes 1573888 | tf_op jit(solution)/shard_map/scatter | solution.py:149
  46.2 9.8 %all-to-all-start.2 = ((bf16[128,2,16,128]{3,2,1,0:T(8,128)(2,1)}), bf16[128,2,16,128]{3,2,1,0:T(8,128)(2,1)S(1)}, u32[]{:S(2)}, u32[]{:S(2)}) async-start(bf16[128,2,16,128]{3,2,1,0:T(8,128)(2,1)} %scatter_fusion.1), calls=%async_computation.2 | async-start | bytes 2097152 | tf_op jit(solution)/shard_map/all_to_all | solution.py:155
  59.2 15.7 %all-to-all-done.2 = bf16[128,2,16,128]{3,2,1,0:T(8,128)(2,1)S(1)} async-done(((bf16[128,2,16,128]{3,2,1,0:T(8,128)(2,1)}), bf16[128,2,16,128]{3,2,1,0:T(8,128)(2,1)S(1)}, u32[]{:S(2)}, u32[]{:S(2)}) %all-to-all-start.2) | async-done | bytes 1048608 | tf_op jit(solution)/shard_map/all_to_all | solution.py:155
  79.8 9.2 %scatter_fusion.2 = f32[128,16,128]{2,1,0:T(8,128)S(1)} fusion(f32[128,16,128]{2,1,0:T(8,128)S(1)} %broadcast_in_dim.43, s32[256]{0:T(256)S(1)} %bitcast.183, f32[256,16,128]{2,1,0:T(8,128)S(1)} %bitcast_convert_fusion), kind=kCustom, calls=%fused_computation.5 | custom fusion | flops 524288 | bytes 6292480 | tf_op jit(solution)/shard_map/scatter-add | solution.py:159
  90.0 13.2 %scatter_fusion.3 = bf16[128,16,128]{2,1,0:T(8,128)(2,1)} fusion(bf16[128,16,128]{2,1,0:T(8,128)(2,1)} %broadcast.194.clone, s32[128]{0:T(128)S(1)} %get-tuple-element.48, bf16[128,16,128]{2,1,0:T(8,128)(2,1)S(1)} %convert_element_type.45), kind=kCustom, calls=%fused_computation.6 | custom fusion | bytes 1573376 | tf_op jit(solution)/shard_map/scatter | solution.py:165
  103.1 9.8 %all-to-all-start.3 = ((bf16[128,16,128]{2,1,0:T(8,128)(2,1)}), bf16[128,16,128]{2,1,0:T(8,128)(2,1)S(1)}, u32[]{:S(2)}, u32[]{:S(2)}) async-start(bf16[128,16,128]{2,1,0:T(8,128)(2,1)} %scatter_fusion.3), calls=%async_computation.3 | async-start | bytes 1048576 | tf_op jit(solution)/shard_map/all_to_all | solution.py:168
  115.7 10.9 %all-to-all-done.3 = bf16[128,16,128]{2,1,0:T(8,128)(2,1)S(1)} async-done(((bf16[128,16,128]{2,1,0:T(8,128)(2,1)}), bf16[128,16,128]{2,1,0:T(8,128)(2,1)S(1)}, u32[]{:S(2)}, u32[]{:S(2)}) %all-to-all-start.3) | async-done | bytes 524320 | tf_op jit(solution)/shard_map/all_to_all | solution.py:168
  142.3 23.1 %all-gather = bf16[16,1,5760]{2,1,0:T(2,128)(2,1)} all-gather(bf16[1,1,5760]{2,1,0:T(2,128)(2,1)S(1)} %reshape.282), channel_id=1, replica_groups=mesh['face'=8,'tile'=16] {'tile'}, dimensions={0}, use_global_device_ids=true | all-gather | bytes 195840 | tf_op jit(solution)/shard_map/all_gather | solution.py:180
  201.9 25.2 %all-gather.6.cloned.1.call-done = bf16[1474560]{0:T(1024)(128)(2,1)} async-done(((bf16[184320]{0:T(1024)(128)(2,1)}), bf16[1474560]{0:T(1024)(128)(2,1)}) %all-gather.6.cloned.1.call-update) | async-done | bytes 2949136 | tf_op jit(solution)/shard_map/all_gather | solution.py:186
  236.0 8.5 %rev.3 = bf16[4,90,512]{2,1,0:T(8,128)(2,1)} reverse(bf16[4,90,512]{2,1,0:T(8,128)(2,1)} %gather_fusion.1), dimensions={2} | reverse | bytes 737280 | tf_op jit(solution)/shard_map/rev | solution.py:191
  251.2 8.4 %maximum_convert_fusion = f32[90,34,514]{2,1,0:T(8,128)} fusion(bf16[90,34,1]{2,1,0:T(8,128)(2,1)} %copy.94, bf16[90,1,512]{2,1,0:T(2,128)(2,1)S(1)} %copy.91, bf16[90,32,512]{2,1,0:T(8,128)(2,1)S(1)} %copy-done.6, bf16[90,1,512]{2,1,0:T(2,128)(2,1)S(1)} %copy.90, bf16[90,34,1]{2,1,0:T(8,128)(2,1)} %copy.93), kind=kLoop, calls=%fused_computation.45 | loop fusion | flops 15728400 | bytes 9437040 | tf_op jit(solution)/shard_map/convert_element_type | solution.py:50
  259.5 34.7 %fusion.38 = (f32[32,512]{1,0:T(8,128)S(1)}, f32[90,32,512]{2,1,0:T(8,128)}) fusion(f32[90,34,514]{2,1,0:T(8,128)} %maximum_convert_fusion, f32[90]{0:T(128)S(1)} %get-tuple-element.43, f32[90]{0:T(128)S(1)} %get-tuple-element.44, f32[90]{0:T(128)S(1)} %get-tuple-element.37, f32[90]{0:T(128)S(1)} %get-tuple-element.38, f32[90]{0:T(128)S(1)} %get-tuple-element.39, ...), kind=kLoop, calls=%fused_computation.128 | loop fusion | flops 26525696 | bytes 59051176 | tf_op jit(solution)/shard_map/reduce_sum | solution.py:58
  303.1 15.2 %multiply_convert_fusion = (bf16[360,16384]{1,0:T(8,128)(2,1)}, f32[16384,360]{0,1:T(8,128)}) fusion(f32[360]{0:T(512)S(1)} %copy-done.18, bf16[90,360]{1,0:T(8,128)(2,1)S(1)} %copy-done.9, f32[90,16384]{1,0:T(8,128)S(1)} %bitcast.150, f32[90]{0:T(128)S(1)} %copy-done.17, f32[90]{0:T(128)S(1)} %copy-done.12, f32[16384]{0:T(1024)S(1)} %bitcast.169, ...), kind=kOutput, calls=%fused_computation.18 | convolution fusion | flops 1128038400 | bytes 41485712 | tf_op jit(solution)/shard_map/dot_general | solution.py:64
  318.3 20.7 %fusion.6 = bf16[360,16384]{1,0:T(8,128)(2,1)} fusion(f32[16384,360]{0,1:T(8,128)} %get-tuple-element.50, bf16[360,90]{0,1:T(8,128)(2,1)S(1)} %copy-done.10, bf16[90,16384]{1,0:T(8,128)(2,1)S(1)} %bitcast.165), kind=kOutput, calls=%fused_computation.16 | convolution fusion | flops 1173749760 | bytes 38403360 | tf_op jit(solution)/shard_map/dot_general | solution.py:75
  339.0 8.7 %convolution_multiply_fusion.1 = f32[90,360]{1,0:T(8,128)} fusion(bf16[360,16384]{1,0:T(8,128)(2,1)} %fusion.6, f32[90,16384]{1,0:T(8,128)S(1)} %bitcast.151, f32[90]{0:T(128)S(1)} %copy-done.17, f32[90]{0:T(128)S(1)} %copy-done.12, f32[16384]{0:T(1024)S(1)} %bitcast.170, f32[16384]{0:T(1024)S(1)} %bitcast.174), kind=kOutput, calls=%fused_computation.48 | convolution fusion | flops 1069088384 | bytes 17956112 | tf_op jit(solution)/shard_map/dot_general | solution.py:41
  347.8 10.4 %fusion.13 = (f32[16384]{0:T(1024)S(1)}, f32[16384,90]{0,1:T(8,128)}) fusion(f32[90,16384]{1,0:T(8,128)S(1)} %bitcast.152, f32[16384]{0:T(1024)S(1)} %bitcast.171, f32[16384]{0:T(1024)S(1)} %bitcast.175, f32[90]{0:T(128)S(1)} %copy-done.12, bf16[360,16384]{1,0:T(8,128)(2,1)} %fusion.6, bf16[90,360]{1,0:T(8,128)(2,1)S(1)} %copy-done.9), kind=kOutput, calls=%fused_computation.31 | convolution fusion | flops 1069039616 | bytes 23854728 | tf_op jit(solution)/shard_map/dot_general | solution.py:78
  358.1 8.7 %convolution_multiply_fusion.2 = f32[360,90]{0,1:T(8,128)} fusion(bf16[360,16384]{1,0:T(8,128)(2,1)} %get-tuple-element.49, bf16[90,16384]{1,0:T(8,128)(2,1)S(1)} %bitcast.166), kind=kOutput, calls=%fused_computation.49 | convolution fusion | flops 1061715584 | bytes 14875200 | tf_op jit(solution)/shard_map/dot_general | solution.py:41
  376.2 7.3 %copy.108 = f32[12,8,32,512]{3,2,1,0:T(8,128)} copy(f32[12,8,32,512]{3,1,2,0:T(8,128)S(1)} %bitcast.158) | data formatting | bytes 12582912
  383.5 31.6 %multiply_reduce_fusion = (f32[90]{0:T(128)S(1)}, f32[90]{0:T(128)S(1)}, f32[90]{0:T(128)S(1)}, f32[90]{0:T(128)S(1)}, f32[90]{0:T(128)S(1)}, /*index=5*/f32[90]...) fusion(f32[90,34,514]{2,1,0:T(8,128)} %maximum_convert_fusion, f32[96,32,512]{2,1,0:T(8,128)} %bitcast.159), kind=kLoop, calls=%fused_computation.34 | loop fusion | flops 26541270 | bytes 58985640 | tf_op jit(solution)/shard_map/reduce_sum | solution.py:90
  423.6 15.7 %psum.46 = f32[9,90]{1,0:T(8,128)S(1)} all-reduce(f32[9,90]{1,0:T(8,128)S(1)} %broadcast_multiply_fusion.3), channel_id=1, replica_groups=mesh['face'=8,'tile'=16] {'face'}, use_global_device_ids=true, to_apply=%region_25.26 | all-reduce | flops 810 | bytes 6480 | tf_op jit(solution)/shard_map/psum | solution.py:211
  439.4 40.0 %psum.47 = f32[9,90]{1,0:T(8,128)} all-reduce(f32[9,90]{1,0:T(8,128)S(1)} %psum.46), channel_id=1, replica_groups=mesh['face'=8,'tile'=16] {'tile'}, use_global_device_ids=true, to_apply=%region_26.27 | all-reduce | flops 810 | bytes 6480 | tf_op jit(solution)/shard_map/psum | solution.py:210
  479.3 7.4 %all-reduce.8.cloned.1.call-done = (f32[90,360]{1,0:T(8,128)}, f32[360,90]{0,1:T(8,128)}) async-done(((f32[90,360]{1,0:T(8,128)}, f32[360,90]{0,1:T(8,128)}), (f32[90,360]{1,0:T(8,128)}, f32[360,90]{0,1:T(8,128)})) %all-reduce.8.cloned.1.call-update) | async-done | bytes 259216 | tf_op jit(solution)/shard_map/psum | solution.py:211
  488.6 137.2 %all-reduce.6.cloned.1.call-done = (f32[90,360]{1,0:T(8,128)}, f32[360,90]{0,1:T(8,128)}) async-done(((f32[90,360]{1,0:T(8,128)}, f32[360,90]{0,1:T(8,128)}), (f32[90,360]{1,0:T(8,128)}, f32[360,90]{0,1:T(8,128)})) %all-reduce.6.cloned.1.call-update) | async-done | bytes 259216 | tf_op jit(solution)/shard_map/psum | solution.py:210
  (150 shorter events, 125.0 us)
Async XLA Ops:
  7.2 20.5 %copy-start = (bf16[64,16,128]{2,1,0:T(8,128)(2,1)S(1)}, bf16[64,16,128]{2,1,0:T(8,128)(2,1)}, u32[]{:S(2)}) copy-start(bf16[64,16,128]{2,1,0:T(8,128)(2,1)} %param.16) | copy-start | bytes 786436
  8.0 48.0 %copy-start.19 = (s32[128]{0:T(128)S(1)}, s32[128]{0:T(128)}, u32[]{:S(2)}) copy-start(s32[128]{0:T(128)} %param.20) | copy-start | bytes 1540
  15.5 30.7 %all-to-all-start.1 = ((s32[128,1,2]{2,1,0:T(1,128)}), s32[128,1,2]{2,1,0:T(1,128)S(1)}, u32[]{:S(2)}, u32[]{:S(2)}) async-start(s32[128,1,2]{2,1,0:T(1,128)} %copy.79), calls=%async_computation.1 | async-start | bytes 131072 | tf_op jit(solution)/shard_map/all_to_all | solution.py:156
  46.2 28.7 %all-to-all-start.2 = ((bf16[128,2,16,128]{3,2,1,0:T(8,128)(2,1)}), bf16[128,2,16,128]{3,2,1,0:T(8,128)(2,1)S(1)}, u32[]{:S(2)}, u32[]{:S(2)}) async-start(bf16[128,2,16,128]{3,2,1,0:T(8,128)(2,1)} %scatter_fusion.1), calls=%async_computation.2 | async-start | bytes 2097152 | tf_op jit(solution)/shard_map/all_to_all | solution.py:155
  74.9 28.2 %all-to-all-start = ((s32[128,1,1]{2,1,0:T(1,128)}), s32[128,1,1]{2,1,0:T(1,128)S(1)}, u32[]{:S(2)}, u32[]{:S(2)}) async-start(s32[128,1,1]{2,1,0:T(1,128)} %copy.78), calls=%async_computation | async-start | bytes 131072 | tf_op jit(solution)/shard_map/all_to_all | solution.py:169
  79.8 51.2 %copy-start.14 = (bf16[16,90]{1,0:T(8,128)(2,1)S(1)}, bf16[16,90]{1,0:T(8,128)(2,1)}, u32[]{:S(2)}) copy-start(bf16[16,90]{1,0:T(8,128)(2,1)} %param.22) | copy-start | bytes 8644
  79.8 51.2 %copy-start.16 = (f32[90]{0:T(128)S(1)}, f32[90]{0:T(128)}, u32[]{:S(2)}) copy-start(f32[90]{0:T(128)} %param.23) | copy-start | bytes 1084
  103.1 23.4 %all-to-all-start.3 = ((bf16[128,16,128]{2,1,0:T(8,128)(2,1)}), bf16[128,16,128]{2,1,0:T(8,128)(2,1)S(1)}, u32[]{:S(2)}, u32[]{:S(2)}) async-start(bf16[128,16,128]{2,1,0:T(8,128)(2,1)} %scatter_fusion.3), calls=%async_computation.3 | async-start | bytes 1048576 | tf_op jit(solution)/shard_map/all_to_all | solution.py:168
  113.0 66.9 %all-gather.4.cloned.1.call-start = ((), (), s32[]{:S(2)}) async-start(), calls=%async_computation.4 | async-start | bytes 1566720 | tf_op jit(solution)/shard_map/all_gather | solution.py:179
  135.9 52.4 %copy-start.11 = (s32[8,4,3]{0,1,2:T(4,128)S(1)}, s32[8,4,3]{0,1,2:T(4,128)}, u32[]{:S(2)}) copy-start(s32[8,4,3]{0,1,2:T(4,128)} %param.21) | copy-start | bytes 1156
  136.7 90.4 %all-gather.6.cloned.1.call-start = ((), (), s32[]{:S(2)}) async-start(), calls=%async_computation.5 | async-start | bytes 3317760 | tf_op jit(solution)/shard_map/all_gather | solution.py:186
  187.7 299.0 %all-reduce.8.cloned.1.call-start = ((), (), s32[]{:S(2)}) async-start(), calls=%async_computation.7 | async-start | bytes 589824 | tf_op jit(solution)/shard_map/psum | solution.py:211
  190.8 9.0 %copy-start.8 = (bf16[90,1,512]{2,0,1:T(8,128)(2,1)S(1)}, bf16[90,1,512]{2,0,1:T(8,128)(2,1)}, u32[]{:S(2)}) copy-start(bf16[90,1,512]{2,0,1:T(8,128)(2,1)} %get-tuple-element.21) | copy-start | bytes 276484
  196.8 51.5 %collective-permute-start = (bf16[90,1,512]{2,0,1:T(8,128)(2,1)}, bf16[90,1,512]{2,0,1:T(8,128)(2,1)S(1)}, u32[]{:S(2)}, u32[]{:S(2)}) collective-permute-start(bf16[90,1,512]{2,0,1:T(8,128)(2,1)} %get-tuple-element.20), channel_id=1, source_target_pairs={{0,1},{1,2},{2,3},{3,4},{4,5},{5,6},{6,7},{7,8},{8,9},{9,10},{10,1... | collective-permute-start | bytes 276488 | tf_op jit(solution)/shard_map/ppermute | solution.py:21
  199.7 51.4 %copy-start.6 = (bf16[90,32,512]{2,1,0:T(8,128)(2,1)S(1)}, bf16[90,32,512]{2,1,0:T(8,128)(2,1)}, u32[]{:S(2)}) copy-start(bf16[90,32,512]{2,1,0:T(8,128)(2,1)} %slice.204) | copy-start | bytes 8847364
  199.7 48.5 %collective-permute-start.1 = (bf16[90,1,512]{2,0,1:T(8,128)(2,1)S(1)}, bf16[90,1,512]{2,0,1:T(8,128)(2,1)S(1)}, u32[]{:S(2)}, u32[]{:S(2)}) collective-permute-start(bf16[90,1,512]{2,0,1:T(8,128)(2,1)S(1)} %copy-done.8), channel_id=1, source_target_pairs={{1,0},{2,1},{3,2},{4,3},{5,4},{6,5},{7,6},{8,7},{9,8},{10,9},{11,1... | collective-permute-start | bytes 276488 | tf_op jit(solution)/shard_map/ppermute | solution.py:23
  294.2 8.0 %slice-start = ((s8[5898240]{0:T(1024)(128)(4,1)}), s8[4194304]{0:T(1024)(128)(4,1)S(1)}, s32[]{:S(2)}) async-start(s8[5898240]{0:T(1024)(128)(4,1)} %bitcast.154), calls=%async_computation.8 | async-start | bytes 8388608
  302.2 45.6 %copy-start.2 = (f32[12,8,32,512]{3,1,2,0:T(8,128)}, f32[12,8,32,512]{3,1,2,0:T(8,128)S(1)}, u32[]{:S(2)}) copy-start(f32[12,8,32,512]{3,1,2,0:T(8,128)S(1)} %copy.103) | copy-start | bytes 18874372
  303.1 15.2 %copy-start.5 = (bf16[12,8,32,512]{3,1,2,0:T(8,128)(2,1)S(1)}, bf16[12,8,32,512]{3,1,2,0:T(8,128)(2,1)}, u32[]{:S(2)}) copy-start(bf16[12,8,32,512]{3,1,2,0:T(8,128)(2,1)} %copy.107) | copy-start | bytes 9437188
  303.1 15.2 %copy-start.10 = (bf16[360,90]{0,1:T(8,128)(2,1)S(1)}, bf16[360,90]{0,1:T(8,128)(2,1)}, u32[]{:S(2)}) copy-start(bf16[360,90]{0,1:T(8,128)(2,1)} %param.29) | copy-start | bytes 194404
  383.5 31.8 %copy-start.4 = (bf16[16384,90]{0,1:T(8,128)(2,1)S(1)}, bf16[16384,90]{0,1:T(8,128)(2,1)}, u32[]{:S(2)}) copy-start(bf16[16384,90]{0,1:T(8,128)(2,1)} %copy-done.3) | copy-start | bytes 8847364
  383.5 31.9 %copy-start.13 = (f32[90]{0:T(128)S(1)}, f32[90]{0:T(128)}, u32[]{:S(2)}) copy-start(f32[90]{0:T(128)} %param.30) | copy-start | bytes 1084
  415.1 210.6 %all-reduce.6.cloned.1.call-start = ((), (), s32[]{:S(2)}) async-start(), calls=%async_computation.6 | async-start | bytes 589824 | tf_op jit(solution)/shard_map/psum | solution.py:210
  422.3 206.6 %copy-start.1 = (bf16[64,16,128]{2,1,0:T(8,128)(2,1)S(1)}, bf16[64,16,128]{2,1,0:T(8,128)(2,1)}, u32[]{:S(2)}) copy-start(bf16[64,16,128]{2,1,0:T(8,128)(2,1)} %param.16) | copy-start | bytes 786436
  (8 other events, 17.9 us)
Sparse Core Ops, SparseCore 0:
  136.8 43.0 all-gather.3
  187.8 39.2 all-gather.5
  415.2 71.4 all-reduce.7
  489.3 136.4 all-reduce.5
